TPU v7x, 32 devices: a whole 2x2x4 slice. The times are simulated.
32 devices in a mesh: blk: 16 (over z, x, core), uly: 2 (over y).
Axes of the slice: x: 2, y: 2, z: 4, core: 2. Of those that a mesh axis runs over, the one named last changes fastest.
Arguments:
- queries: bfloat16 [16384, 1024], P(('blk', 'uly')), may hold values from -6 to 6
- key_states: bfloat16 [16384, 128], P(('blk', 'uly')), may hold values from -6 to 6
- value_states: bfloat16 [16384, 128], P(('blk', 'uly')), may hold values from -6 to 6
- attn_output: bfloat16 [16384, 1024], P(('blk', 'uly')), may hold values from -6 to 6
- grad_output: bfloat16 [16384, 1024], P(('blk', 'uly')), may hold values from -6 to 6
- log_normalizer: float32 [8, 16384], P(None, ('blk', 'uly')), may hold values from 0 to 12
- span_order: int32 [32], replicated, may hold values from 0 to 31, as said below
Outputs:
- grad_queries: bfloat16 [16384, 1024], P(('blk', 'uly'))
- grad_keys: bfloat16 [16384, 128], P(('blk', 'uly'))
- grad_values: bfloat16 [16384, 128], P(('blk', 'uly'))
Inputs may be any that keep to these rules, and one draw needn't show every extreme that they name: `span_order`: every value appears once; for every b, entries 2b and 2b+1 lie in sequence b mod 1 (value // 32) and sum to (2 * (b mod 1) + 1) * 2 * 16 - 1.
All inputs are finite; a program needn't handle non-finite values.
Results may differ from a plain program's by a relative error of at most 0.0051.
Values may be sent and summed in bfloat16 or wider, within the bound.
A program may use at most 64 MiB of HBM per device.

v0:
```python
import functools
import math

import jax
import jax.numpy as jnp
from jax import lax
from jax.experimental import pallas as pl
from jax.experimental.pallas import tpu as pltpu
from jax.sharding import PartitionSpec as P

CYCLE = 16
SUB = 256
CHUNKS = 2
ORDER_A = (2, 4, 1, 8, 16)
ORDER_B = (2, 1, 8, 16, 4)
BOTH = ("blk", "uly")


def dot(a, b):
    return lax.dot_general(a, b, (((1,), (0,)), ((), ())), preferred_element_type=jnp.float32)


def tile_kernel(
    heads, span, head_dim, plan, kv_ref, qt_ref, dt_ref, q_ref, do_ref, lse_ref, delta_ref, dqi_ref, da_ref, db_ref, dq_ref
):
    step = pl.program_id(0)
    rows = kv_ref.shape[0]
    half = rows // 2
    scaling = 1.0 / math.sqrt(head_dim)
    to_log2 = math.log2(math.e) * scaling
    sub = min(SUB, span)

    @pl.when(step == 0)
    def _():
        dq_ref[...] = dqi_ref[...]

    def tile(part, diagonal):
        key = kv_ref[:, :head_dim]
        value = kv_ref[:, head_dim:]
        key_t = key.T
        dk = jnp.zeros((rows, head_dim), jnp.float32)
        dv = jnp.zeros((rows, head_dim), jnp.float32)
        for h in range(heads):
            hs = slice(h * head_dim, (h + 1) * head_dim)
            for s in range(span // sub):
                qs = slice(part * span + s * sub, part * span + (s + 1) * sub)
                scores = dot(key, qt_ref[hs, qs])
                dprobs = dot(value, dt_ref[hs, qs])
                probs = jnp.exp2(scores * to_log2 - lse_ref[h : h + 1, qs])
                if diagonal:
                    q_at = lax.broadcasted_iota(jnp.int32, (rows, sub), 1) + s * sub
                    k_at = lax.broadcasted_iota(jnp.int32, (rows, sub), 0) + plan[2, step]
                    probs = jnp.where(q_at >= k_at, probs, 0.0)
                dscores = (scaling * probs * (dprobs - delta_ref[h : h + 1, qs])).astype(jnp.bfloat16)
                dv = dv + dot(probs.astype(jnp.bfloat16), do_ref[qs, hs])
                dk = dk + dot(dscores, q_ref[qs, hs])
                dq_ref[hs, qs] += dot(key_t, dscores)
        return jnp.concatenate([dk, dv], axis=1)

    def put(total):
        da_ref[...] = total[:half].astype(da_ref.dtype)
        db_ref[...] = total[half:].astype(db_ref.dtype)

    da_ref[...] = jnp.zeros_like(da_ref)
    db_ref[...] = jnp.zeros_like(db_ref)
    for part in range(2):
        for kind in (1, 2):

            @pl.when(plan[part, step] == kind)
            def _():
                so_far = jnp.concatenate([da_ref[...], db_ref[...]], axis=0).astype(jnp.float32)
                put(so_far + tile(part, kind == 1))


def attend(plan, kv, rows, q_t, d_t, q, do, lse, delta, dq_in, span, kind):
    heads = lse.shape[0]
    head_dim = kv.shape[1] // 2
    blocks = kv.shape[0] // rows
    whole = lambda a: pl.BlockSpec(a.shape, lambda n, plan: (0, 0))
    ops = (q_t, d_t, q, do, lse, delta, dq_in)
    out = jax.ShapeDtypeStruct((kv.shape[0] // 2, 2 * head_dim), kind)
    work = 10 * 2 * span * heads * head_dim * kv.shape[0]
    return pl.pallas_call(
        functools.partial(tile_kernel, heads, span, head_dim),
        grid_spec=pltpu.PrefetchScalarGridSpec(
            num_scalar_prefetch=1,
            grid=(blocks,),
            in_specs=[pl.BlockSpec((rows, 2 * head_dim), lambda n, plan: (plan[3, n], 0))] + [whole(a) for a in ops],
            out_specs=[
                pl.BlockSpec((rows // 2, 2 * head_dim), lambda n, plan: (n, 0)),
                pl.BlockSpec((rows // 2, 2 * head_dim), lambda n, plan: (plan[4, n], 0)),
                whole(dq_in),
            ],
        ),
        out_shape=[out, out, jax.ShapeDtypeStruct(dq_in.shape, jnp.float32)],
        compiler_params=pltpu.CompilerParams(vmem_limit_bytes=48 * 2**20),
        cost_estimate=pl.CostEstimate(flops=work, bytes_accessed=4 * kv.size, transcendentals=0),
    )(plan, kv, *ops)


def swap(value, mask):
    if mask == 1:
        return lax.ppermute(value, "uly", [(0, 1), (1, 0)])
    count = lax.axis_size("blk")
    return lax.ppermute(value, "blk", [(b, b ^ (mask // 2)) for b in range(count)])


def halve(parts, order):
    keep = parts
    for mask in order:
        half = keep.shape[0] // 2
        sent = swap(keep[half:].astype(jnp.bfloat16), mask)
        keep = keep[:half].astype(jnp.float32) + sent.astype(jnp.float32)
    return keep


def spot(order, mask):
    bits = len(order)
    return sum(1 << (bits - 1 - i) for i, m in enumerate(order) if mask & m)


def body(queries, key_states, value_states, attn_output, grad_output, log_normalizer, span_order):
    local = queries.shape[0]
    heads = log_normalizer.shape[0]
    head_dim = key_states.shape[1]
    n_blk, n_uly = lax.axis_size("blk"), lax.axis_size("uly")
    count = n_blk * n_uly
    span = local * n_uly // 2
    seq_spans = span_order.shape[0] // (n_blk // CYCLE)
    folding = n_uly == 2 and n_blk == 16
    chunks = CHUNKS
    rows = local // chunks
    kv_local = jnp.concatenate([key_states, value_states], axis=1)
    kvs = [lax.all_gather(kv_local[c * rows : (c + 1) * rows], BOTH, axis=0, tiled=True) for c in range(chunks)]

    delta_local = jnp.sum(
        (attn_output.astype(jnp.float32) * grad_output.astype(jnp.float32)).reshape(local, heads, head_dim), axis=2
    ).T
    q = lax.all_to_all(queries, "uly", split_axis=1, concat_axis=0, tiled=True)
    do = lax.all_to_all(grad_output, "uly", split_axis=1, concat_axis=0, tiled=True)
    rows_in = jnp.stack([log_normalizer * math.log2(math.e), delta_local], axis=1)
    rows_group = lax.all_to_all(rows_in, "uly", split_axis=0, concat_axis=2, tiled=True)
    lse, delta = rows_group[:, 0], rows_group[:, 1]

    me = lax.axis_index("blk")
    mine = lax.dynamic_slice(span_order, (2 * me,), (2,))
    if folding:
        masks = [0] * count
        for mask in range(count):
            masks[spot(ORDER_A, mask)] = mask
        device = (me * n_uly + lax.axis_index("uly")) ^ jnp.array(masks, jnp.int32)
        second = jnp.array([spot(ORDER_B, mask) for mask in masks], jnp.int32)
    else:
        device = jnp.arange(count, dtype=jnp.int32)
        second = device
    start = (device % n_uly) * local
    block_span = span_order[2 * (device // n_uly) + start // span]
    same = (block_span // seq_spans)[None] == (mine // seq_spans)[:, None]
    order = jnp.where(mine[:, None] > block_span[None], 2, jnp.where(mine[:, None] == block_span[None], 1, 0))
    order = jnp.where(same, order, 0)

    q_t, d_t = q.T, do.T
    dq_t = jnp.zeros((q.shape[1], q.shape[0]), jnp.float32)
    totals = []
    for c in range(chunks):
        plan = jnp.concatenate([order, jnp.stack([start % span + c * rows, device, second])], axis=0).astype(jnp.int32)
        first, other, dq_t = attend(
            plan, kvs[c], rows, q_t, d_t, q, do, lse, delta, dq_t, span, jnp.bfloat16 if folding else jnp.float32
        )
        if folding:
            split = (count, rows // 2, 2 * head_dim)
            totals.append(halve(first.reshape(split), ORDER_A)[0])
            totals.append(halve(other.reshape(split), ORDER_B)[0])
        else:
            totals.append(lax.psum_scatter(first, BOTH, scatter_dimension=0, tiled=True))
            totals.append(lax.psum_scatter(other, BOTH, scatter_dimension=0, tiled=True))
    grad_queries = lax.all_to_all(dq_t.T.astype(jnp.bfloat16), "uly", split_axis=0, concat_axis=1, tiled=True)
    total = jnp.concatenate(totals, axis=0).astype(jnp.bfloat16)
    return (grad_queries, total[:, :head_dim], total[:, head_dim:])


def solution(mesh):
    return jax.shard_map(
        body,
        mesh=mesh,
        in_specs=(
            P(BOTH, None),
            P(BOTH, None),
            P(BOTH, None),
            P(BOTH, None),
            P(BOTH, None),
            P(None, BOTH),
            P(),
        ),
        out_specs=(P(BOTH, None), P(BOTH, None), P(BOTH, None)),
        check_vma=False,
    )
```

profile of v0, /device:TPU:0, one launch (start us, length us, event | category | flops | bytes accessed | tf_op | source)
XLA Modules:
  0.0 334.0 jit_solution(12091265189164069354)
XLA Ops:
  7.2 0.9 constant_dynamic-update-slice_fusion.1
  8.1 0.9 constant_dynamic-update-slice_fusion
  10.6 1.9 multiply_bitcast_fusion
  14.7 1.0 multiply_bitcast_fusion.1
  16.5 4.2 %all-to-all-start.2 = ((f32[8,2,512]{2,1,0:T(2,128)}), f32[8,2,512]{2,1,0:T(2,128)S(1)}, u32[]{:S(2)}, u32[]{:S(2)}) async-start(f32[8,2,512]{2,1,0:T(2,128)} %copy.53), calls=%async_computation.2 | async-start | bytes 65536 | tf_op jit(solution)/shard_map/all_to_all | solution.py:142
  20.8 1.1 copy.71
  21.8 2.9 all-to-all-done.2
  24.7 3.7 %all-to-all-start = ((bf16[512,2,512]{2,0,1:T(8,128)(2,1)}), bf16[512,2,512]{2,0,1:T(8,128)(2,1)S(1)}, u32[]{:S(2)}, u32[]{:S(2)}) async-start(bf16[512,2,512]{2,0,1:T(8,128)(2,1)} %bitcast.68), calls=%async_computation | async-start | bytes 2097152 | tf_op jit(solution)/shard_map/all_to_all | solution.py:139
  28.4 1.0 copy.70
  30.3 11.1 %all-to-all-done = bf16[512,2,512]{2,0,1:T(8,128)(2,1)S(1)} async-done(((bf16[512,2,512]{2,0,1:T(8,128)(2,1)}), bf16[512,2,512]{2,0,1:T(8,128)(2,1)S(1)}, u32[]{:S(2)}, u32[]{:S(2)}) %all-to-all-start) | async-done | bytes 1048608 | tf_op jit(solution)/shard_map/all_to_all | solution.py:139
  41.3 3.6 %all-to-all-start.1 = ((bf16[512,2,512]{2,0,1:T(8,128)(2,1)}), bf16[512,2,512]{2,0,1:T(8,128)(2,1)S(1)}, u32[]{:S(2)}, u32[]{:S(2)}) async-start(bf16[512,2,512]{2,0,1:T(8,128)(2,1)} %bitcast.67), calls=%async_computation.1 | async-start | bytes 2097152 | tf_op jit(solution)/shard_map/all_to_all | solution.py:140
  45.7 11.3 %all-to-all-done.1 = bf16[512,2,512]{2,0,1:T(8,128)(2,1)S(1)} async-done(((bf16[512,2,512]{2,0,1:T(8,128)(2,1)}), bf16[512,2,512]{2,0,1:T(8,128)(2,1)S(1)}, u32[]{:S(2)}, u32[]{:S(2)}) %all-to-all-start.1) | async-done | bytes 1048608 | tf_op jit(solution)/shard_map/all_to_all | solution.py:140
  56.9 1.3 copy.58.dt_ref
  58.3 18.1 %all-gather.5.cloned.1.call-done.kv_ref = bf16[8192,256]{1,0:T(8,128)(2,1)} async-done(((bf16[256,256]{1,0:T(8,128)(2,1)}), bf16[8192,256]{1,0:T(8,128)(2,1)}) %all-gather.5.cloned.1.call-update) | async-done | bytes 4194320 | tf_op jit(solution)/shard_map/all_gather | solution.py:134
  76.3 1.6 broadcast_in_dim.30.dqi_ref
  77.9 77.9 %shard_map.112 = (bf16[4096,256]{1,0:T(8,128)(2,1)}, bf16[4096,256]{1,0:T(8,128)(2,1)}, f32[512,1024]{1,0:T(8,128)}) custom-call(s32[5,32]{1,0:T(8,128)S(1)} %get-tuple-element.43.plan, bf16[8192,256]{1,0:T(8,128)(2,1)} %all-gather.5.cloned.1.call-done.kv_ref, bf16[512,1024]{1,0:T(8,128)(2,1)S(1)} %copy.57.qt_ref, bf16[512,1024]{1,0:T(8,128)(2,1)S(1)} %copy-done, ...), custom_call_target="tpu_custom_call" | custom-call | flops 42949672960 | bytes 8388608 | tf_op jit(solution)/shard_map/pallas_call | solution.py:83
  155.8 4.2 %fusion.10 = (bf16[2048,256]{1,0:T(8,128)(2,1)}, bf16[2048,256]{1,0:T(8,128)(2,1)}, bf16[2048,256]{1,0:T(8,128)(2,1)}, bf16[2048,256]{1,0:T(8,128)(2,1)}) fusion(bf16[4096,256]{1,0:T(8,128)(2,1)} %get-tuple-element.11, bf16[4096,256]{1,0:T(8,128)(2,1)} %get-tuple-element.12), kind=kLoop, calls=%fused_computation.91 | loop fusion | bytes 8388608 | tf_op jit(solution)/shard_map/slice | solution.py:112
  160.0 5.1 %collective-permute-start = (bf16[16,128,256]{2,1,0:T(8,128)(2,1)}, bf16[16,128,256]{2,1,0:T(8,128)(2,1)}, u32[]{:S(2)}, u32[]{:S(2)}) collective-permute-start(bf16[16,128,256]{2,1,0:T(8,128)(2,1)} %bitcast.22), channel_id=1, source_target_pairs={{0,2},{2,0},{4,6},{6,4},{8,10},{10,8},{12,14},{14,12},{16,18},{18,... | collective-permute-start | bytes 3145736 | tf_op jit(solution)/shard_map/ppermute | solution.py:105
  165.1 1.2 copy-done.1
  166.3 78.2 %shard_map.113 = (bf16[4096,256]{1,0:T(8,128)(2,1)}, bf16[4096,256]{1,0:T(8,128)(2,1)}, f32[512,1024]{1,0:T(8,128)}) custom-call(s32[5,32]{1,0:T(8,128)S(1)} %get-tuple-element.44.plan, bf16[8192,256]{1,0:T(8,128)(2,1)} %all-gather.3.cloned.1.call-done.kv_ref, bf16[512,1024]{1,0:T(8,128)(2,1)S(1)} %copy.57.qt_ref, bf16[512,1024]{1,0:T(8,128)(2,1)S(1)} %copy-done.1, ...), custom_call_target="tpu_custom_call" | custom-call | flops 42949672960 | bytes 8388608 | tf_op jit(solution)/shard_map/pallas_call | solution.py:83
  244.5 1.7 convert_element_type.115
  246.2 1.0 copy.69
  247.3 3.6 %all-to-all-start.3 = ((bf16[2,512,512]{1,2,0:T(8,128)(2,1)}), bf16[2,512,512]{1,2,0:T(8,128)(2,1)S(1)}, u32[]{:S(2)}, u32[]{:S(2)}) async-start(bf16[2,512,512]{1,2,0:T(8,128)(2,1)} %bitcast.66), calls=%async_computation.3 | async-start | bytes 2097152 | tf_op jit(solution)/shard_map/all_to_all | solution.py:177
  250.9 3.9 %fusion.12 = (bf16[2048,256]{1,0:T(8,128)(2,1)}, bf16[2048,256]{1,0:T(8,128)(2,1)}, bf16[2048,256]{1,0:T(8,128)(2,1)S(1)}, bf16[2048,256]{1,0:T(8,128)(2,1)}) fusion(bf16[4096,256]{1,0:T(8,128)(2,1)} %get-tuple-element.13, bf16[4096,256]{1,0:T(8,128)(2,1)} %get-tuple-element.14), kind=kLoop, calls=%fused_computation.93 | loop fusion | bytes 8388608 | tf_op jit(solution)/shard_map/slice | solution.py:112
  254.8 5.9 %collective-permute-start.10 = (bf16[16,128,256]{2,1,0:T(8,128)(2,1)}, bf16[16,128,256]{2,1,0:T(8,128)(2,1)}, u32[]{:S(2)}, u32[]{:S(2)}) collective-permute-start(bf16[16,128,256]{2,1,0:T(8,128)(2,1)} %bitcast.28), channel_id=1, source_target_pairs={{0,2},{2,0},{4,6},{6,4},{8,10},{10,8},{12,14},{14,12},{16,18},{18,... | collective-permute-start | bytes 3145736 | tf_op jit(solution)/shard_map/ppermute | solution.py:105
  260.7 1.3 copy.60
  262.0 1.6 convert_add_fusion.3
  263.7 1.6 convert_add_fusion.2
  265.3 2.7 collective-permute-start.6
  268.0 1.5 convert_add_fusion.1
  269.6 2.1 collective-permute-start.11
  271.6 1.5 convert_add_fusion
  273.3 0.9 collective-permute-done.1
  274.3 5.3 %collective-permute-start.2 = (bf16[4,128,256]{2,1,0:T(8,128)(2,1)S(1)}, bf16[4,128,256]{2,1,0:T(8,128)(2,1)S(1)}, u32[]{:S(2)}, u32[]{:S(2)}) collective-permute-start(bf16[4,128,256]{2,1,0:T(8,128)(2,1)S(1)} %slice.317), channel_id=1, source_target_pairs={{0,1},{1,0},{2,3},{3,2},{4,5},{5,4},{6,7},{7,6},{8,9},{9,8},{10,11... | collective-permute-start | bytes 786440 | tf_op jit(solution)/shard_map/ppermute | solution.py:103
  279.8 8.6 %collective-permute-start.7 = (bf16[4,128,256]{2,1,0:T(8,128)(2,1)S(1)}, bf16[4,128,256]{2,1,0:T(8,128)(2,1)S(1)}, u32[]{:S(2)}, u32[]{:S(2)}) collective-permute-start(bf16[4,128,256]{2,1,0:T(8,128)(2,1)S(1)} %slice.316), channel_id=1, source_target_pairs={{0,8},{2,10},{4,12},{6,14},{8,0},{10,2},{12,4},{14,6},{16,24},{18,... | collective-permute-start | bytes 786440 | tf_op jit(solution)/shard_map/ppermute | solution.py:105
  288.5 2.3 collective-permute-start.12
  291.0 8.6 %collective-permute-start.17 = (bf16[4,128,256]{2,1,0:T(8,128)(2,1)S(1)}, bf16[4,128,256]{2,1,0:T(8,128)(2,1)S(1)}, u32[]{:S(2)}, u32[]{:S(2)}) collective-permute-start(bf16[4,128,256]{2,1,0:T(8,128)(2,1)S(1)} %slice.314), channel_id=1, source_target_pairs={{0,8},{2,10},{4,12},{6,14},{8,0},{10,2},{12,4},{14,6},{16,24},{18,... | collective-permute-start | bytes 786440 | tf_op jit(solution)/shard_map/ppermute | solution.py:105
  299.7 4.0 %collective-permute-start.3 = (bf16[2,128,256]{2,1,0:T(8,128)(2,1)S(1)}, bf16[2,128,256]{2,1,0:T(8,128)(2,1)S(1)}, u32[]{:S(2)}, u32[]{:S(2)}) collective-permute-start(bf16[2,128,256]{2,1,0:T(8,128)(2,1)S(1)} %slice.321), channel_id=1, source_target_pairs={{0,8},{2,10},{4,12},{6,14},{8,0},{10,2},{12,4},{14,6},{16,24},{18,... | collective-permute-start | bytes 393224 | tf_op jit(solution)/shard_map/ppermute | solution.py:105
  303.8 0.8 collective-permute-start.8
  304.7 1.8 collective-permute-start.13
  306.6 3.6 %collective-permute-start.18 = (bf16[2,128,256]{2,1,0:T(8,128)(2,1)S(1)}, bf16[2,128,256]{2,1,0:T(8,128)(2,1)S(1)}, u32[]{:S(2)}, u32[]{:S(2)}) collective-permute-start(bf16[2,128,256]{2,1,0:T(8,128)(2,1)S(1)} %slice.318), channel_id=1, source_target_pairs={{0,16},{2,18},{4,20},{6,22},{8,24},{10,26},{12,28},{14,30},{16,0},... | collective-permute-start | bytes 393224 | tf_op jit(solution)/shard_map/ppermute | solution.py:105
  310.4 2.9 collective-permute-done.8
  313.3 2.3 collective-permute-start.9
  315.7 1.6 collective-permute-start.14
  317.2 4.4 %collective-permute-done.18 = bf16[2,128,256]{2,1,0:T(8,128)(2,1)S(1)} collective-permute-done((bf16[2,128,256]{2,1,0:T(8,128)(2,1)S(1)}, bf16[2,128,256]{2,1,0:T(8,128)(2,1)S(1)}, u32[]{:S(2)}, u32[]{:S(2)}) %collective-permute-start.18) | collective-permute-done | bytes 131104 | tf_op jit(solution)/shard_map/ppermute | solution.py:105
  321.7 1.0 collective-permute-start.19
  323.1 1.4 collective-permute-done.14
  324.5 1.9 collective-permute-done.19
  (99 shorter events, 8.7 us)
Async XLA Ops:
  7.2 69.1 %all-gather.5.cloned.1.call-start = ((), (), s32[]{:S(2)}) async-start(), calls=%async_computation.5 | async-start | bytes 4325376 | tf_op jit(solution)/shard_map/all_gather | solution.py:134
  9.8 155.2 %all-gather.3.cloned.1.call-start = ((), (), s32[]{:S(2)}) async-start(), calls=%async_computation.4 | async-start | bytes 4325376 | tf_op jit(solution)/shard_map/all_gather | solution.py:134
  12.5 0.7 copy-start.8
  14.1 6.7 %copy-start.9 = (s32[32]{0:T(128)S(1)}, s32[32]{0:T(128)}, u32[]{:S(2)}) copy-start(s32[32]{0:T(128)} %constant.95.clone) | copy-start | bytes 388
  14.1 6.7 %copy-start.7 = (bf16[512,1024]{1,0:T(8,128)(2,1)S(1)}, bf16[512,1024]{1,0:T(8,128)(2,1)}, u32[]{:S(2)}) copy-start(bf16[512,1024]{1,0:T(8,128)(2,1)} %param.9) | copy-start | bytes 3145732
  16.5 8.2 %all-to-all-start.2 = ((f32[8,2,512]{2,1,0:T(2,128)}), f32[8,2,512]{2,1,0:T(2,128)S(1)}, u32[]{:S(2)}, u32[]{:S(2)}) async-start(f32[8,2,512]{2,1,0:T(2,128)} %copy.53), calls=%async_computation.2 | async-start | bytes 65536 | tf_op jit(solution)/shard_map/all_to_all | solution.py:142
  20.8 7.7 %copy-start.3 = (bf16[512,1024]{1,0:T(8,128)(2,1)S(1)}, bf16[512,1024]{1,0:T(8,128)(2,1)}, u32[]{:S(2)}) copy-start(bf16[512,1024]{1,0:T(8,128)(2,1)} %param.13) | copy-start | bytes 3145732
  24.7 4.8 %copy-start.2 = (s32[32]{0:T(128)S(1)}, s32[32]{0:T(128)}, u32[]{:S(2)}) copy-start(s32[32]{0:T(128)} %param.15) | copy-start | bytes 388
  24.7 16.7 %all-to-all-start = ((bf16[512,2,512]{2,0,1:T(8,128)(2,1)}), bf16[512,2,512]{2,0,1:T(8,128)(2,1)S(1)}, u32[]{:S(2)}, u32[]{:S(2)}) async-start(bf16[512,2,512]{2,0,1:T(8,128)(2,1)} %bitcast.68), calls=%async_computation | async-start | bytes 2097152 | tf_op jit(solution)/shard_map/all_to_all | solution.py:139
  28.4 16.6 %copy-start.10 = (s32[1,32]{1,0:T(1,128)S(1)}, s32[1,32]{1,0:T(1,128)}, u32[]{:S(2)}) copy-start(s32[1,32]{1,0:T(1,128)} %constant.97) | copy-start | bytes 388
  41.3 15.6 %all-to-all-start.1 = ((bf16[512,2,512]{2,0,1:T(8,128)(2,1)}), bf16[512,2,512]{2,0,1:T(8,128)(2,1)S(1)}, u32[]{:S(2)}, u32[]{:S(2)}) async-start(bf16[512,2,512]{2,0,1:T(8,128)(2,1)} %bitcast.67), calls=%async_computation.1 | async-start | bytes 2097152 | tf_op jit(solution)/shard_map/all_to_all | solution.py:140
  76.3 1.6 copy-start
  160.0 102.0 %collective-permute-start = (bf16[16,128,256]{2,1,0:T(8,128)(2,1)}, bf16[16,128,256]{2,1,0:T(8,128)(2,1)}, u32[]{:S(2)}, u32[]{:S(2)}) collective-permute-start(bf16[16,128,256]{2,1,0:T(8,128)(2,1)} %bitcast.22), channel_id=1, source_target_pairs={{0,2},{2,0},{4,6},{6,4},{8,10},{10,8},{12,14},{14,12},{16,18},{18,... | collective-permute-start | bytes 3145736 | tf_op jit(solution)/shard_map/ppermute | solution.py:105
  165.0 98.6 %collective-permute-start.5 = (bf16[16,128,256]{2,1,0:T(8,128)(2,1)}, bf16[16,128,256]{2,1,0:T(8,128)(2,1)}, u32[]{:S(2)}, u32[]{:S(2)}) collective-permute-start(bf16[16,128,256]{2,1,0:T(8,128)(2,1)} %bitcast.25), channel_id=1, source_target_pairs={{0,2},{2,0},{4,6},{6,4},{8,10},{10,8},{12,14},{14,12},{16,18},{18,... | collective-permute-start | bytes 3145736 | tf_op jit(solution)/shard_map/ppermute | solution.py:105
  165.1 1.2 copy-start.1
  247.3 13.4 %all-to-all-start.3 = ((bf16[2,512,512]{1,2,0:T(8,128)(2,1)}), bf16[2,512,512]{1,2,0:T(8,128)(2,1)S(1)}, u32[]{:S(2)}, u32[]{:S(2)}) async-start(bf16[2,512,512]{1,2,0:T(8,128)(2,1)} %bitcast.66), calls=%async_computation.3 | async-start | bytes 2097152 | tf_op jit(solution)/shard_map/all_to_all | solution.py:177
  254.8 7.2 %copy-start.5 = (bf16[2048,256]{1,0:T(8,128)(2,1)S(1)}, bf16[2048,256]{1,0:T(8,128)(2,1)}, u32[]{:S(2)}) copy-start(bf16[2048,256]{1,0:T(8,128)(2,1)} %get-tuple-element.30) | copy-start | bytes 3145732
  254.8 13.3 %collective-permute-start.10 = (bf16[16,128,256]{2,1,0:T(8,128)(2,1)}, bf16[16,128,256]{2,1,0:T(8,128)(2,1)}, u32[]{:S(2)}, u32[]{:S(2)}) collective-permute-start(bf16[16,128,256]{2,1,0:T(8,128)(2,1)} %bitcast.28), channel_id=1, source_target_pairs={{0,2},{2,0},{4,6},{6,4},{8,10},{10,8},{12,14},{14,12},{16,18},{18,... | collective-permute-start | bytes 3145736 | tf_op jit(solution)/shard_map/ppermute | solution.py:105
  260.6 11.0 %collective-permute-start.15 = (bf16[16,128,256]{2,1,0:T(8,128)(2,1)}, bf16[16,128,256]{2,1,0:T(8,128)(2,1)}, u32[]{:S(2)}, u32[]{:S(2)}) collective-permute-start(bf16[16,128,256]{2,1,0:T(8,128)(2,1)} %bitcast.31), channel_id=1, source_target_pairs={{0,2},{2,0},{4,6},{6,4},{8,10},{10,8},{12,14},{14,12},{16,18},{18,... | collective-permute-start | bytes 3145736 | tf_op jit(solution)/shard_map/ppermute | solution.py:105
  262.0 1.7 copy-start.4
  263.6 10.6 %collective-permute-start.1 = (bf16[8,128,256]{2,1,0:T(8,128)(2,1)S(1)}, bf16[8,128,256]{2,1,0:T(8,128)(2,1)S(1)}, u32[]{:S(2)}, u32[]{:S(2)}) collective-permute-start(bf16[8,128,256]{2,1,0:T(8,128)(2,1)S(1)} %slice.313), channel_id=1, source_target_pairs={{0,4},{2,6},{4,0},{6,2},{8,12},{10,14},{12,8},{14,10},{16,20},{18,... | collective-permute-start | bytes 1572872 | tf_op jit(solution)/shard_map/ppermute | solution.py:105
  263.7 4.3 %copy-start.6 = (bf16[2048,256]{1,0:T(8,128)(2,1)S(1)}, bf16[2048,256]{1,0:T(8,128)(2,1)}, u32[]{:S(2)}) copy-start(bf16[2048,256]{1,0:T(8,128)(2,1)} %get-tuple-element.34) | copy-start | bytes 3145732
  265.3 14.3 %collective-permute-start.6 = (bf16[8,128,256]{2,1,0:T(8,128)(2,1)S(1)}, bf16[8,128,256]{2,1,0:T(8,128)(2,1)S(1)}, u32[]{:S(2)}, u32[]{:S(2)}) collective-permute-start(bf16[8,128,256]{2,1,0:T(8,128)(2,1)S(1)} %slice.312), channel_id=1, source_target_pairs={{0,1},{1,0},{2,3},{3,2},{4,5},{5,4},{6,7},{7,6},{8,9},{9,8},{10,11... | collective-permute-start | bytes 1572872 | tf_op jit(solution)/shard_map/ppermute | solution.py:103
  269.6 18.8 %collective-permute-start.11 = (bf16[8,128,256]{2,1,0:T(8,128)(2,1)S(1)}, bf16[8,128,256]{2,1,0:T(8,128)(2,1)S(1)}, u32[]{:S(2)}, u32[]{:S(2)}) collective-permute-start(bf16[8,128,256]{2,1,0:T(8,128)(2,1)S(1)} %slice.311), channel_id=1, source_target_pairs={{0,4},{2,6},{4,0},{6,2},{8,12},{10,14},{12,8},{14,10},{16,20},{18,... | collective-permute-start | bytes 1572872 | tf_op jit(solution)/shard_map/ppermute | solution.py:105
  273.2 17.7 %collective-permute-start.16 = (bf16[8,128,256]{2,1,0:T(8,128)(2,1)S(1)}, bf16[8,128,256]{2,1,0:T(8,128)(2,1)S(1)}, u32[]{:S(2)}, u32[]{:S(2)}) collective-permute-start(bf16[8,128,256]{2,1,0:T(8,128)(2,1)S(1)} %slice.310), channel_id=1, source_target_pairs={{0,1},{1,0},{2,3},{3,2},{4,5},{5,4},{6,7},{7,6},{8,9},{9,8},{10,11... | collective-permute-start | bytes 1572872 | tf_op jit(solution)/shard_map/ppermute | solution.py:103
  274.3 25.3 %collective-permute-start.2 = (bf16[4,128,256]{2,1,0:T(8,128)(2,1)S(1)}, bf16[4,128,256]{2,1,0:T(8,128)(2,1)S(1)}, u32[]{:S(2)}, u32[]{:S(2)}) collective-permute-start(bf16[4,128,256]{2,1,0:T(8,128)(2,1)S(1)} %slice.317), channel_id=1, source_target_pairs={{0,1},{1,0},{2,3},{3,2},{4,5},{5,4},{6,7},{7,6},{8,9},{9,8},{10,11... | collective-permute-start | bytes 786440 | tf_op jit(solution)/shard_map/ppermute | solution.py:103
  279.8 23.9 %collective-permute-start.7 = (bf16[4,128,256]{2,1,0:T(8,128)(2,1)S(1)}, bf16[4,128,256]{2,1,0:T(8,128)(2,1)S(1)}, u32[]{:S(2)}, u32[]{:S(2)}) collective-permute-start(bf16[4,128,256]{2,1,0:T(8,128)(2,1)S(1)} %slice.316), channel_id=1, source_target_pairs={{0,8},{2,10},{4,12},{6,14},{8,0},{10,2},{12,4},{14,6},{16,24},{18,... | collective-permute-start | bytes 786440 | tf_op jit(solution)/shard_map/ppermute | solution.py:105
  288.5 16.1 %collective-permute-start.12 = (bf16[4,128,256]{2,1,0:T(8,128)(2,1)S(1)}, bf16[4,128,256]{2,1,0:T(8,128)(2,1)S(1)}, u32[]{:S(2)}, u32[]{:S(2)}) collective-permute-start(bf16[4,128,256]{2,1,0:T(8,128)(2,1)S(1)} %slice.315), channel_id=1, source_target_pairs={{0,1},{1,0},{2,3},{3,2},{4,5},{5,4},{6,7},{7,6},{8,9},{9,8},{10,11... | collective-permute-start | bytes 786440 | tf_op jit(solution)/shard_map/ppermute | solution.py:103
  291.0 15.5 %collective-permute-start.17 = (bf16[4,128,256]{2,1,0:T(8,128)(2,1)S(1)}, bf16[4,128,256]{2,1,0:T(8,128)(2,1)S(1)}, u32[]{:S(2)}, u32[]{:S(2)}) collective-permute-start(bf16[4,128,256]{2,1,0:T(8,128)(2,1)S(1)} %slice.314), channel_id=1, source_target_pairs={{0,8},{2,10},{4,12},{6,14},{8,0},{10,2},{12,4},{14,6},{16,24},{18,... | collective-permute-start | bytes 786440 | tf_op jit(solution)/shard_map/ppermute | solution.py:105
  299.7 10.5 %collective-permute-start.3 = (bf16[2,128,256]{2,1,0:T(8,128)(2,1)S(1)}, bf16[2,128,256]{2,1,0:T(8,128)(2,1)S(1)}, u32[]{:S(2)}, u32[]{:S(2)}) collective-permute-start(bf16[2,128,256]{2,1,0:T(8,128)(2,1)S(1)} %slice.321), channel_id=1, source_target_pairs={{0,8},{2,10},{4,12},{6,14},{8,0},{10,2},{12,4},{14,6},{16,24},{18,... | collective-permute-start | bytes 393224 | tf_op jit(solution)/shard_map/ppermute | solution.py:105
  303.8 9.5 %collective-permute-start.8 = (bf16[2,128,256]{2,1,0:T(8,128)(2,1)S(1)}, bf16[2,128,256]{2,1,0:T(8,128)(2,1)S(1)}, u32[]{:S(2)}, u32[]{:S(2)}) collective-permute-start(bf16[2,128,256]{2,1,0:T(8,128)(2,1)S(1)} %slice.320), channel_id=1, source_target_pairs={{0,16},{2,18},{4,20},{6,22},{8,24},{10,26},{12,28},{14,30},{16,0},... | collective-permute-start | bytes 393224 | tf_op jit(solution)/shard_map/ppermute | solution.py:105
  304.7 10.9 %collective-permute-start.13 = (bf16[2,128,256]{2,1,0:T(8,128)(2,1)S(1)}, bf16[2,128,256]{2,1,0:T(8,128)(2,1)S(1)}, u32[]{:S(2)}, u32[]{:S(2)}) collective-permute-start(bf16[2,128,256]{2,1,0:T(8,128)(2,1)S(1)} %slice.319), channel_id=1, source_target_pairs={{0,8},{2,10},{4,12},{6,14},{8,0},{10,2},{12,4},{14,6},{16,24},{18,... | collective-permute-start | bytes 393224 | tf_op jit(solution)/shard_map/ppermute | solution.py:105
  306.6 15.1 %collective-permute-start.18 = (bf16[2,128,256]{2,1,0:T(8,128)(2,1)S(1)}, bf16[2,128,256]{2,1,0:T(8,128)(2,1)S(1)}, u32[]{:S(2)}, u32[]{:S(2)}) collective-permute-start(bf16[2,128,256]{2,1,0:T(8,128)(2,1)S(1)} %slice.318), channel_id=1, source_target_pairs={{0,16},{2,18},{4,20},{6,22},{8,24},{10,26},{12,28},{14,30},{16,0},... | collective-permute-start | bytes 393224 | tf_op jit(solution)/shard_map/ppermute | solution.py:105
  310.3 12.8 %collective-permute-start.4 = (bf16[1,128,256]{2,1,0:T(8,128)(2,1)S(1)}, bf16[1,128,256]{2,1,0:T(8,128)(2,1)S(1)}, u32[]{:S(2)}, u32[]{:S(2)}) collective-permute-start(bf16[1,128,256]{2,1,0:T(8,128)(2,1)S(1)} %slice.325), channel_id=1, source_target_pairs={{0,16},{2,18},{4,20},{6,22},{8,24},{10,26},{12,28},{14,30},{16,0},... | collective-permute-start | bytes 196616 | tf_op jit(solution)/shard_map/ppermute | solution.py:105
  313.3 9.7 %collective-permute-start.9 = (bf16[1,128,256]{2,1,0:T(8,128)(2,1)S(1)}, bf16[1,128,256]{2,1,0:T(8,128)(2,1)S(1)}, u32[]{:S(2)}, u32[]{:S(2)}) collective-permute-start(bf16[1,128,256]{2,1,0:T(8,128)(2,1)S(1)} %slice.324), channel_id=1, source_target_pairs={{0,4},{2,6},{4,0},{6,2},{8,12},{10,14},{12,8},{14,10},{16,20},{18,... | collective-permute-start | bytes 196616 | tf_op jit(solution)/shard_map/ppermute | solution.py:105
  315.7 8.8 %collective-permute-start.14 = (bf16[1,128,256]{2,1,0:T(8,128)(2,1)S(1)}, bf16[1,128,256]{2,1,0:T(8,128)(2,1)S(1)}, u32[]{:S(2)}, u32[]{:S(2)}) collective-permute-start(bf16[1,128,256]{2,1,0:T(8,128)(2,1)S(1)} %slice.323), channel_id=1, source_target_pairs={{0,16},{2,18},{4,20},{6,22},{8,24},{10,26},{12,28},{14,30},{16,0},... | collective-permute-start | bytes 196616 | tf_op jit(solution)/shard_map/ppermute | solution.py:105
  321.7 4.7 %collective-permute-start.19 = (bf16[1,128,256]{2,1,0:T(8,128)(2,1)S(1)}, bf16[1,128,256]{2,1,0:T(8,128)(2,1)S(1)}, u32[]{:S(2)}, u32[]{:S(2)}) collective-permute-start(bf16[1,128,256]{2,1,0:T(8,128)(2,1)S(1)} %slice.322), channel_id=1, source_target_pairs={{0,4},{2,6},{4,0},{6,2},{8,12},{10,14},{12,8},{14,10},{16,20},{18,... | collective-permute-start | bytes 196616 | tf_op jit(solution)/shard_map/ppermute | solution.py:105
Sparse Core Ops, SparseCore 0:
  11.5 64.8 all-gather.4
  79.8 60.6 all-gather.2
where the time goes:
time: 337 us; the launch traced here: 334 us
  Pallas kernels  156 us (46%)
  starting transfers between devices  71.1 us (21%)
  waiting for transfers between devices  55.8 us (17%)
  local copies, waits for them, and re-layouts  24 us (7%)
  between operations  14.5 us (4%)
  other arithmetic  12.4 us (4%)
    pallas_call x2, Pallas kernels, attend(): pl.pallas_call(functools.partial(tile_kernel, heads, span, head_dim), gri...  156 us
    ppermute x16, starting transfers between devices, swap(): lax.ppermute(value, 'blk', [(b, b ^ mask // 2) for b in range(count)])  45.5 us
    all_gather x2, waiting for transfers between devices, body(): lax.all_gather(kv_local[c * rows:(c + 1) * rows], BOTH, axis=0, tiled=True)  18.1 us
    ppermute x16, waiting for transfers between devices, swap(): lax.ppermute(value, 'blk', [(b, b ^ mask // 2) for b in range(count)])  11.8 us
    all_to_all x1, waiting for transfers between devices, body(): lax.all_to_all(grad_output, 'uly', split_axis=1, concat_axis=0, tiled=True)  11.3 us
    all_to_all x1, waiting for transfers between devices, body(): q = lax.all_to_all(queries, 'uly', split_axis=1, concat_axis=0, tiled=True)  11.1 us
    ppermute x4, starting transfers between devices, swap(): return lax.ppermute(value, 'uly', [(0, 1), (1, 0)])  10.4 us
    slice x18, local copies, waits for them, and re-layouts, halve(): sent = swap(keep[half:].astype(jnp.bfloat16), mask)  8.49 us
  transfers between devices with their start and end apart: 26, of which 10 were waited for; matrix products, arithmetic and copies ran while one was open for 9% of the time, Pallas kernels for 47%

commit v1 on v0

v1 whole, which is shorter than its diff:
```python
import functools
import math

import jax
import jax.numpy as jnp
from jax import lax
from jax.experimental import pallas as pl
from jax.experimental.pallas import tpu as pltpu
from jax.sharding import PartitionSpec as P

CYCLE = 16
SUB = 256
ORDER = (2, 4, 1)
TURNS = (1, 2, 3, 0)
BOTH = ("blk", "uly")


def dot(a, b):
    return lax.dot_general(a, b, (((1,), (0,)), ((), ())), preferred_element_type=jnp.float32)


def tile_kernel(
    heads, span, head_dim, apart, plan, kv_ref, qt_ref, dt_ref, q_ref, do_ref, lse_ref, delta_ref, dqi_ref, *refs
):
    dq_ref, acc = refs[-2:]
    dkv_refs = refs[-2 - apart : -2]
    step = pl.program_id(0)
    rows = kv_ref.shape[0]
    scaling = 1.0 / math.sqrt(head_dim)
    to_log2 = math.log2(math.e) * scaling
    sub = min(SUB, span)

    @pl.when(step == 0)
    def _():
        dq_ref[...] = dqi_ref[...]

    def tile(part, diagonal):
        key = kv_ref[:, :head_dim]
        value = kv_ref[:, head_dim:]
        key_t = key.T
        dk = jnp.zeros((rows, head_dim), jnp.float32)
        dv = jnp.zeros((rows, head_dim), jnp.float32)
        for h in range(heads):
            hs = slice(h * head_dim, (h + 1) * head_dim)
            for s in range(span // sub):
                qs = slice(part * span + s * sub, part * span + (s + 1) * sub)
                scores = dot(key, qt_ref[hs, qs])
                dprobs = dot(value, dt_ref[hs, qs])
                probs = jnp.exp2(scores * to_log2 - lse_ref[h : h + 1, qs])
                if diagonal:
                    q_at = lax.broadcasted_iota(jnp.int32, (rows, sub), 1) + s * sub
                    k_at = lax.broadcasted_iota(jnp.int32, (rows, sub), 0) + plan[2, step]
                    probs = jnp.where(q_at >= k_at, probs, 0.0)
                dscores = (scaling * probs * (dprobs - delta_ref[h : h + 1, qs])).astype(jnp.bfloat16)
                dv = dv + dot(probs.astype(jnp.bfloat16), do_ref[qs, hs])
                dk = dk + dot(dscores, q_ref[qs, hs])
                dq_ref[hs, qs] += dot(key_t, dscores)
        acc[:, :head_dim] += dk
        acc[:, head_dim:] += dv

    acc[...] = jnp.zeros_like(acc)
    for part in range(2):
        for kind in (1, 2):

            @pl.when(plan[part, step] == kind)
            def _():
                tile(part, kind == 1)

    if apart == 1:
        dkv_refs[0][...] = acc[...].astype(dkv_refs[0].dtype)
    else:
        for n in range(apart):

            @pl.when(step == n)
            def _():
                dkv_refs[n][...] = acc[...].astype(dkv_refs[n].dtype)


def attend(plan, kv, rows, q_t, d_t, q, do, lse, delta, dq_in, span, apart, kind, after=()):
    heads = lse.shape[0]
    head_dim = kv.shape[1] // 2
    blocks = kv.shape[0] // rows
    whole = lambda a: pl.BlockSpec(a.shape, lambda n, plan: (0, 0))
    ops = (q_t, d_t, q, do, lse, delta, dq_in)
    kv_shape = (rows, 2 * head_dim)
    if apart == 1:
        kv_out = [pl.BlockSpec(kv_shape, lambda n, plan: (n, 0))]
        kv_shape = kv.shape
    else:
        kv_out = [pl.BlockSpec(kv_shape, lambda n, plan: (0, 0))] * apart
    work = 10 * 2 * span * heads * head_dim * kv.shape[0]
    return pl.pallas_call(
        functools.partial(tile_kernel, heads, span, head_dim, apart),
        grid_spec=pltpu.PrefetchScalarGridSpec(
            num_scalar_prefetch=1,
            grid=(blocks,),
            in_specs=[pl.BlockSpec((rows, 2 * head_dim), lambda n, plan: (plan[3, n], 0))]
            + [whole(a) for a in ops]
            + [pl.BlockSpec(memory_space=pl.ANY) for _ in after],
            out_specs=kv_out + [whole(dq_in)],
            scratch_shapes=[pltpu.VMEM((rows, 2 * head_dim), jnp.float32)],
        ),
        out_shape=[jax.ShapeDtypeStruct(kv_shape, kind)] * apart + [jax.ShapeDtypeStruct(dq_in.shape, jnp.float32)],
        compiler_params=pltpu.CompilerParams(vmem_limit_bytes=48 * 2**20),
        cost_estimate=pl.CostEstimate(flops=work, bytes_accessed=4 * kv.size, transcendentals=0),
    )(plan, kv, *ops, *after)


def swap(value, mask):
    count, sides = lax.axis_size("blk"), lax.axis_size("uly")
    return lax.ppermute(value, BOTH, [(d, d ^ mask) for d in range(count * sides)])


def make_plan(device, mine, span_order, local, span, spot):
    n_blk, n_uly = lax.axis_size("blk"), lax.axis_size("uly")
    seq_spans = span_order.shape[0] // (n_blk // CYCLE)
    start = (device % n_uly) * local
    block_span = span_order[2 * (device // n_uly) + start // span]
    same = (block_span // seq_spans)[None] == (mine // seq_spans)[:, None]
    order = jnp.where(mine[:, None] > block_span[None], 2, jnp.where(mine[:, None] == block_span[None], 1, 0))
    order = jnp.where(same, order, 0)
    return jnp.concatenate([order, jnp.stack([start % span, spot])], axis=0).astype(jnp.int32)


def body(queries, key_states, value_states, attn_output, grad_output, log_normalizer, span_order):
    local = queries.shape[0]
    heads = log_normalizer.shape[0]
    head_dim = key_states.shape[1]
    n_blk, n_uly = lax.axis_size("blk"), lax.axis_size("uly")
    count = n_blk * n_uly
    span = local * n_uly // 2
    plane = 2 ** len(ORDER)
    folding = n_uly == 2 and n_blk == 16
    me, side = lax.axis_index("blk"), lax.axis_index("uly")
    delta_local = jnp.sum(
        (attn_output.astype(jnp.float32) * grad_output.astype(jnp.float32)).reshape(local, heads, head_dim), axis=2
    ).T
    rows_in = jnp.stack([log_normalizer * math.log2(math.e), delta_local], axis=1)
    kv_local = jnp.concatenate([key_states, value_states], axis=1)
    pair = lax.dynamic_slice(span_order, (2 * me,), (2,))

    if folding:
        groups = [list(range(g, g + plane // 2)) for g in range(0, n_blk, plane // 2)]

        kv_pair = jnp.concatenate([kv_local, swap(kv_local, 1)], axis=0)

        def gather(k):
            block = swap(kv_pair, k * plane) if k else kv_pair
            return lax.all_gather(block, "blk", axis=0, tiled=True, axis_index_groups=groups)

        kvs = [gather(k) for k in TURNS]

        def share(value, axis):
            size = value.shape[axis] // 2
            own = lax.dynamic_slice_in_dim(value, side * size, size, axis)
            other = swap(lax.dynamic_slice_in_dim(value, (1 - side) * size, size, axis), 1)
            return own, other

        lines = jnp.concatenate(share(rows_in, 0), axis=2)
        q = jnp.concatenate(share(queries, 1), axis=0)
        do = jnp.concatenate(share(grad_output, 1), axis=0)
        mine = jnp.where(side == 0, pair, pair[::-1])
    else:
        q = lax.all_to_all(queries, "uly", split_axis=1, concat_axis=0, tiled=True)
        do = lax.all_to_all(grad_output, "uly", split_axis=1, concat_axis=0, tiled=True)
        lines = lax.all_to_all(rows_in, "uly", split_axis=0, concat_axis=2, tiled=True)
        mine = pair
    lse, delta = lines[:, 0], lines[:, 1]
    q_t, d_t = q.T, do.T
    dq_t = jnp.zeros((q.shape[1], q.shape[0]), jnp.float32)

    if folding:
        masks = [sum(m for i, m in enumerate(reversed(ORDER)) if n >> i & 1) for n in range(plane)]
        here = me * n_uly + side
        sums = []
        for turn, (k, kv) in enumerate(zip(TURNS, kvs)):
            device = here ^ (jnp.array(masks, jnp.int32) | (k * plane))
            plan = make_plan(device, mine, span_order, local, span, (device % plane) ^ side)
            after = tuple(sums[: turn - 1][-1:]) if turn > 1 else ()
            *parts, dq_t = attend(
                plan, kv, local, q_t, d_t, q, do, lse, delta, dq_t, span, plane, jnp.bfloat16, after
            )
            part = parts[0].astype(jnp.float32)
            for mask, sent in zip(masks[1:], parts[1:]):
                part = part + swap(sent, mask).astype(jnp.float32)
            sums.append(part.astype(jnp.bfloat16) if k else part)
        total = sums[-1]
        for k, part in zip(TURNS[:-1], sums):
            total = total + swap(part, k * plane).astype(jnp.float32)
        back = swap(dq_t[:, local:].T.astype(jnp.bfloat16), 1)
        own = dq_t[:, :local].T.astype(jnp.bfloat16)
        grad_queries = jnp.concatenate(
            [jnp.where(side == 0, own, back), jnp.where(side == 0, back, own)], axis=1
        )
    else:
        kv = lax.all_gather(kv_local, BOTH, axis=0, tiled=True)
        device = jnp.arange(count, dtype=jnp.int32)
        plan = make_plan(device, mine, span_order, local, span, device)
        dkv, dq_t = attend(plan, kv, local, q_t, d_t, q, do, lse, delta, dq_t, span, 1, jnp.float32)
        total = lax.psum_scatter(dkv, BOTH, scatter_dimension=0, tiled=True)
        grad_queries = lax.all_to_all(dq_t.T.astype(jnp.bfloat16), "uly", split_axis=0, concat_axis=1, tiled=True)
    total = total.astype(jnp.bfloat16)
    return (grad_queries, total[:, :head_dim], total[:, head_dim:])


def solution(mesh):
    return jax.shard_map(
        body,
        mesh=mesh,
        in_specs=(
            P(BOTH, None),
            P(BOTH, None),
            P(BOTH, None),
            P(BOTH, None),
            P(BOTH, None),
            P(None, BOTH),
            P(),
        ),
        out_specs=(P(BOTH, None), P(BOTH, None), P(BOTH, None)),
        check_vma=False,
    )
```

time: 337 us -> 317 us (0.941)
  the two profiles are of different devices: /device:TPU:0 before, /device:TPU:11 now
where the time goes in v1:
time: 317 us; the launch traced here: 313 us
  Pallas kernels  116 us (37%)
  waiting for transfers between devices  91.7 us (29%)
  starting transfers between devices  49.3 us (16%)
  local copies, waits for them, and re-layouts  25.1 us (8%)
  other arithmetic  16.5 us (5%)
  between operations  14.6 us (5%)
    pallas_call x4, Pallas kernels, attend(): pl.pallas_call(functools.partial(tile_kernel, heads, span, head_dim, apar...  116 us
    ppermute x39, waiting for transfers between devices, swap(): lax.ppermute(value, BOTH, [(d, d ^ mask) for d in range(count * sides)])  91.6 us
    ppermute x39, starting transfers between devices, swap(): lax.ppermute(value, BOTH, [(d, d ^ mask) for d in range(count * sides)])  49.2 us
    unnamed x81, local copies, waits for them, and re-layouts  14.7 us
  transfers between devices with their start and end apart: 43, of which 12 were waited for; matrix products, arithmetic and copies ran while one was open for 9% of the time, Pallas kernels for 37%

profile of v1, /device:TPU:11, one launch (start us, length us, event | category | flops | bytes accessed | tf_op | source)
XLA Modules:
  0.0 312.9 jit_solution(13460588991796726216)
XLA Ops:
  9.2 1.3 collective-permute-start
  10.5 5.9 %collective-permute-done = bf16[512,256]{1,0:T(8,128)(2,1)S(1)} collective-permute-done((bf16[512,256]{1,0:T(8,128)(2,1)S(1)}, bf16[512,256]{1,0:T(8,128)(2,1)S(1)}, u32[]{:S(2)}, u32[]{:S(2)}) %collective-permute-start) | collective-permute-done | bytes 262176 | tf_op jit(solution)/shard_map/ppermute | solution.py:111
  16.8 11.7 %collective-permute-done.6 = bf16[1024,256]{1,0:T(8,128)(2,1)S(1)} collective-permute-done((bf16[1024,256]{1,0:T(8,128)(2,1)S(1)}, bf16[1024,256]{1,0:T(8,128)(2,1)S(1)}, u32[]{:S(2)}, u32[]{:S(2)}) %collective-permute-start.6) | collective-permute-done | bytes 524320 | tf_op jit(solution)/shard_map/ppermute | solution.py:111
  29.4 2.4 collective-permute-start.5
  31.7 1.1 constant_dynamic-slice_fusion.3
  32.9 1.2 collective-permute-start.1
  34.1 1.1 constant_dynamic-slice_fusion.1
  35.4 19.1 %collective-permute-done.5 = bf16[1024,256]{1,0:T(8,128)(2,1)S(1)} collective-permute-done((bf16[1024,256]{1,0:T(8,128)(2,1)S(1)}, bf16[1024,256]{1,0:T(8,128)(2,1)S(1)}, u32[]{:S(2)}, u32[]{:S(2)}) %collective-permute-start.5) | collective-permute-done | bytes 524320 | tf_op jit(solution)/shard_map/ppermute | solution.py:111
  55.4 1.7 multiply_bitcast_fusion
  57.1 2.1 copy.42
  60.0 1.3 collective-permute-start.3
  64.6 23.5 %collective-permute-done.4 = bf16[1024,256]{1,0:T(8,128)(2,1)S(1)} collective-permute-done((bf16[1024,256]{1,0:T(8,128)(2,1)S(1)}, bf16[1024,256]{1,0:T(8,128)(2,1)S(1)}, u32[]{:S(2)}, u32[]{:S(2)}) %collective-permute-start.4) | collective-permute-done | bytes 524320 | tf_op jit(solution)/shard_map/ppermute | solution.py:111
  89.1 1.2 pad_maximum_fusion
  90.8 2.8 pad_maximum_fusion.1
  93.6 1.5 copy.40.dt_ref
  95.1 1.6 broadcast_in_dim.72.dqi_ref
  96.8 27.4 %shard_map.130 = (bf16[512,256]{1,0:T(8,128)(2,1)S(1)}, bf16[512,256]{1,0:T(8,128)(2,1)S(1)}, bf16[512,256]{1,0:T(8,128)(2,1)S(1)}, bf16[512,256]{1,0:T(8,128)(2...) custom-call(s32[4,8]{1,0:T(4,128)S(1)} %pad_add_fusion.3.plan, ...), custom_call_target="tpu_custom_call" | custom-call | flops 21474836480 | bytes 4194304 | tf_op jit(solution)/shard_map/pallas_call | solution.py:92
  128.4 2.5 collective-permute-start.10
  132.0 1.9 collective-permute-start.13
  135.1 5.0 %collective-permute-done.11 = bf16[512,256]{1,0:T(8,128)(2,1)} collective-permute-done((bf16[512,256]{1,0:T(8,128)(2,1)}, bf16[512,256]{1,0:T(8,128)(2,1)}, u32[]{:S(2)}, u32[]{:S(2)}) %collective-permute-start.11) | collective-permute-done | bytes 262176 | tf_op jit(solution)/shard_map/ppermute | solution.py:111
  140.5 28.9 %shard_map.131 = (bf16[512,256]{1,0:T(8,128)(2,1)S(1)}, bf16[512,256]{1,0:T(8,128)(2,1)S(1)}, bf16[512,256]{1,0:T(8,128)(2,1)S(1)}, bf16[512,256]{1,0:T(8,128)(2...) custom-call(s32[4,8]{1,0:T(4,128)S(1)} %pad_add_fusion.2.plan, ...), custom_call_target="tpu_custom_call" | custom-call | flops 21474836480 | bytes 4194304 | tf_op jit(solution)/shard_map/pallas_call | solution.py:92
  170.9 2.3 collective-permute-start.15
  174.0 1.5 collective-permute-start.18
  175.5 1.7 add_convert_fusion.3.refs_0_
  177.7 1.7 collective-permute-start.19
  180.1 2.5 collective-permute-start.20
  182.7 28.6 %shard_map.132 = (bf16[512,256]{1,0:T(8,128)(2,1)S(1)}, bf16[512,256]{1,0:T(8,128)(2,1)}, bf16[512,256]{1,0:T(8,128)(2,1)}, bf16[512,256]{1,0:T(8,128)(2,1)}, bf...) custom-call(s32[4,8]{1,0:T(4,128)S(1)} %pad_add_fusion.1.plan, ...), custom_call_target="tpu_custom_call" | custom-call | flops 21474836480 | bytes 4194304 | tf_op jit(solution)/shard_map/pallas_call | solution.py:92
  213.4 1.2 collective-permute-start.31
  214.6 2.6 collective-permute-start.32
  217.1 1.2 collective-permute-start.34
  219.1 2.2 add_convert_fusion.2.refs_0_
  221.4 30.8 %shard_map.133 = (bf16[512,256]{1,0:T(8,128)(2,1)S(1)}, bf16[512,256]{1,0:T(8,128)(2,1)S(1)}, bf16[512,256]{1,0:T(8,128)(2,1)S(1)}, bf16[512,256]{1,0:T(8,128)(2...) custom-call(s32[4,8]{1,0:T(4,128)S(1)} %pad_add_fusion.plan, ...), custom_call_target="tpu_custom_call" | custom-call | flops 21474836480 | bytes 4194304 | tf_op jit(solution)/shard_map/pallas_call | solution.py:92
  252.2 1.9 convert.4
  254.1 1.8 collective-permute-start.36
  257.9 2.8 collective-permute-start.23
  260.7 1.1 collective-permute-done.36
  261.7 3.7 %collective-permute-start.24 = (bf16[512,256]{1,0:T(8,128)(2,1)S(1)}, bf16[512,256]{1,0:T(8,128)(2,1)S(1)}, u32[]{:S(2)}, u32[]{:S(2)}) collective-permute-start(bf16[512,256]{1,0:T(8,128)(2,1)S(1)} %get-tuple-element.62), channel_id=1, source_target_pairs={{0,5},{1,4},{2,7},{3,6},{4,1},{5,0},{6,3},{7,2},{8,13},{9,12},{10,... | collective-permute-start | bytes 786440 | tf_op jit(solution)/shard_map/ppermute | solution.py:111
  265.5 2.3 collective-permute-done.37
  267.8 3.1 collective-permute-start.25
  270.8 3.1 collective-permute-start.26
  273.9 2.2 add_convert_fusion.1
  276.2 4.3 %collective-permute-done.24 = bf16[512,256]{1,0:T(8,128)(2,1)S(1)} collective-permute-done((bf16[512,256]{1,0:T(8,128)(2,1)S(1)}, bf16[512,256]{1,0:T(8,128)(2,1)S(1)}, u32[]{:S(2)}, u32[]{:S(2)}) %collective-permute-start.24) | collective-permute-done | bytes 262176 | tf_op jit(solution)/shard_map/ppermute | solution.py:111
  280.6 11.8 %collective-permute-done.26 = bf16[512,256]{1,0:T(8,128)(2,1)S(1)} collective-permute-done((bf16[512,256]{1,0:T(8,128)(2,1)S(1)}, bf16[512,256]{1,0:T(8,128)(2,1)S(1)}, u32[]{:S(2)}, u32[]{:S(2)}) %collective-permute-start.26) | collective-permute-done | bytes 262176 | tf_op jit(solution)/shard_map/ppermute | solution.py:111
  292.4 3.4 %collective-permute-start.28 = (bf16[512,256]{1,0:T(8,128)(2,1)}, bf16[512,256]{1,0:T(8,128)(2,1)}, u32[]{:S(2)}, u32[]{:S(2)}) collective-permute-start(bf16[512,256]{1,0:T(8,128)(2,1)} %get-tuple-element.66), channel_id=1, source_target_pairs={{0,7},{1,6},{2,5},{3,4},{4,3},{5,2},{6,1},{7,0},{8,15},{9,14},{10,... | collective-permute-start | bytes 786440 | tf_op jit(solution)/shard_map/ppermute | solution.py:111
  296.1 1.3 copy.41
  297.4 4.2 %collective-permute-done.28 = bf16[512,256]{1,0:T(8,128)(2,1)} collective-permute-done((bf16[512,256]{1,0:T(8,128)(2,1)}, bf16[512,256]{1,0:T(8,128)(2,1)}, u32[]{:S(2)}, u32[]{:S(2)}) %collective-permute-start.28) | collective-permute-done | bytes 262176 | tf_op jit(solution)/shard_map/ppermute | solution.py:111
  301.6 2.2 collective-permute-done.38
  303.8 1.6 add_convert_fusion
  (177 shorter events, 25.7 us)
Async XLA Ops:
  7.2 87.9 %all-gather.11.cloned.1.call-start = ((), (), s32[]{:S(2)}) async-start(), calls=%async_computation.3 | async-start | bytes 2621440 | tf_op jit(solution)/shard_map/all_gather | solution.py:149
  9.2 7.2 %collective-permute-start = (bf16[512,256]{1,0:T(8,128)(2,1)S(1)}, bf16[512,256]{1,0:T(8,128)(2,1)S(1)}, u32[]{:S(2)}, u32[]{:S(2)}) collective-permute-start(bf16[512,256]{1,0:T(8,128)(2,1)S(1)} %constant_dynamic-update-slice_fusion), channel_id=1, source_target_pairs={{0,1},{1,0},{2,3},{3,2},{4,5},{5,4},{6,7},{7,6},{8,9},{9,8},{10,11... | collective-permute-start | bytes 786440 | tf_op jit(solution)/shard_map/ppermute | solution.py:111
  16.5 47.6 %copy-start.19 = (bf16[1024,256]{1,0:T(8,128)(2,1)}, bf16[1024,256]{1,0:T(8,128)(2,1)S(1)}, u32[]{:S(2)}) copy-start(bf16[1024,256]{1,0:T(8,128)(2,1)S(1)} %pad_maximum_fusion.3) | copy-start | bytes 1572868
  16.5 11.9 %collective-permute-start.6 = (bf16[1024,256]{1,0:T(8,128)(2,1)S(1)}, bf16[1024,256]{1,0:T(8,128)(2,1)S(1)}, u32[]{:S(2)}, u32[]{:S(2)}) collective-permute-start(bf16[1024,256]{1,0:T(8,128)(2,1)S(1)} %pad_maximum_fusion.3), channel_id=1, source_target_pairs={{0,8},{1,9},{2,10},{3,11},{4,12},{5,13},{6,14},{7,15},{8,0},{9,1},... | collective-permute-start | bytes 1572872 | tf_op jit(solution)/shard_map/ppermute | solution.py:111
  29.3 111.2 %all-gather.9.cloned.1.call-start = ((), (), s32[]{:S(2)}) async-start(), calls=%async_computation.2 | async-start | bytes 2621440 | tf_op jit(solution)/shard_map/all_gather | solution.py:149
  29.4 25.1 %collective-permute-start.5 = (bf16[1024,256]{1,0:T(8,128)(2,1)S(1)}, bf16[1024,256]{1,0:T(8,128)(2,1)S(1)}, u32[]{:S(2)}, u32[]{:S(2)}) collective-permute-start(bf16[1024,256]{1,0:T(8,128)(2,1)S(1)} %pad_maximum_fusion.3), channel_id=1, source_target_pairs={{0,16},{1,17},{2,18},{3,19},{4,20},{5,21},{6,22},{7,23},{8,24},{9,... | collective-permute-start | bytes 1572872 | tf_op jit(solution)/shard_map/ppermute | solution.py:111
  32.9 56.2 %collective-permute-start.1 = (bf16[512,512]{1,0:T(8,128)(2,1)}, bf16[512,512]{1,0:T(8,128)(2,1)}, u32[]{:S(2)}, u32[]{:S(2)}) collective-permute-start(bf16[512,512]{1,0:T(8,128)(2,1)} %get-tuple-element.103), channel_id=1, source_target_pairs={{0,1},{1,0},{2,3},{3,2},{4,5},{5,4},{6,7},{7,6},{8,9},{9,8},{10,11... | collective-permute-start | bytes 1572872 | tf_op jit(solution)/shard_map/ppermute | solution.py:111
  35.2 55.6 %collective-permute-start.2 = (bf16[512,512]{1,0:T(8,128)(2,1)}, bf16[512,512]{1,0:T(8,128)(2,1)}, u32[]{:S(2)}, u32[]{:S(2)}) collective-permute-start(bf16[512,512]{1,0:T(8,128)(2,1)} %get-tuple-element.101), channel_id=1, source_target_pairs={{0,1},{1,0},{2,3},{3,2},{4,5},{5,4},{6,7},{7,6},{8,9},{9,8},{10,11... | collective-permute-start | bytes 1572872 | tf_op jit(solution)/shard_map/ppermute | solution.py:111
  55.4 127.3 %all-gather.7.cloned.1.call-start = ((), (), s32[]{:S(2)}) async-start(), calls=%async_computation.1 | async-start | bytes 2621440 | tf_op jit(solution)/shard_map/all_gather | solution.py:149
  60.0 29.0 %collective-permute-start.3 = (f32[4,2,512]{2,0,1:T(4,128)S(1)}, f32[4,2,512]{2,0,1:T(4,128)S(1)}, u32[]{:S(2)}, u32[]{:S(2)}) collective-permute-start(f32[4,2,512]{2,0,1:T(4,128)S(1)} %get-tuple-element.108), channel_id=1, source_target_pairs={{0,1},{1,0},{2,3},{3,2},{4,5},{5,4},{6,7},{7,6},{8,9},{9,8},{10,11... | collective-permute-start | bytes 49160 | tf_op jit(solution)/shard_map/ppermute | solution.py:111
  64.1 24.0 %collective-permute-start.4 = (bf16[1024,256]{1,0:T(8,128)(2,1)S(1)}, bf16[1024,256]{1,0:T(8,128)(2,1)S(1)}, u32[]{:S(2)}, u32[]{:S(2)}) collective-permute-start(bf16[1024,256]{1,0:T(8,128)(2,1)S(1)} %pad_maximum_fusion.3), channel_id=1, source_target_pairs={{0,24},{1,25},{2,26},{3,27},{4,28},{5,29},{6,30},{7,31},{8,16},{9,... | collective-permute-start | bytes 1572872 | tf_op jit(solution)/shard_map/ppermute | solution.py:111
  89.0 132.4 %all-gather.5.cloned.1.call-start = ((), (), s32[]{:S(2)}) async-start(), calls=%async_computation | async-start | bytes 2621440 | tf_op jit(solution)/shard_map/all_gather | solution.py:149
  128.4 6.5 %collective-permute-start.10 = (bf16[512,256]{1,0:T(8,128)(2,1)}, bf16[512,256]{1,0:T(8,128)(2,1)}, u32[]{:S(2)}, u32[]{:S(2)}) collective-permute-start(bf16[512,256]{1,0:T(8,128)(2,1)} %get-tuple-element.45), channel_id=1, source_target_pairs={{0,2},{1,3},{2,0},{3,1},{4,6},{5,7},{6,4},{7,5},{8,10},{9,11},{10,... | collective-permute-start | bytes 786440 | tf_op jit(solution)/shard_map/ppermute | solution.py:111
  130.9 9.2 %collective-permute-start.11 = (bf16[512,256]{1,0:T(8,128)(2,1)}, bf16[512,256]{1,0:T(8,128)(2,1)}, u32[]{:S(2)}, u32[]{:S(2)}) collective-permute-start(bf16[512,256]{1,0:T(8,128)(2,1)} %get-tuple-element.46), channel_id=1, source_target_pairs={{0,3},{1,2},{2,1},{3,0},{4,7},{5,6},{6,5},{7,4},{8,11},{9,10},{10,... | collective-permute-start | bytes 786440 | tf_op jit(solution)/shard_map/ppermute | solution.py:111
  131.9 38.2 %collective-permute-start.12 = (bf16[512,256]{1,0:T(8,128)(2,1)}, bf16[512,256]{1,0:T(8,128)(2,1)}, u32[]{:S(2)}, u32[]{:S(2)}) collective-permute-start(bf16[512,256]{1,0:T(8,128)(2,1)} %copy-done.16), channel_id=1, source_target_pairs={{0,6},{1,7},{2,4},{3,5},{4,2},{5,3},{6,0},{7,1},{8,14},{9,15},{10,... | collective-permute-start | bytes 786440 | tf_op jit(solution)/shard_map/ppermute | solution.py:111
  132.0 38.9 %collective-permute-start.13 = (bf16[512,256]{1,0:T(8,128)(2,1)}, bf16[512,256]{1,0:T(8,128)(2,1)}, u32[]{:S(2)}, u32[]{:S(2)}) collective-permute-start(bf16[512,256]{1,0:T(8,128)(2,1)} %copy-done.15), channel_id=1, source_target_pairs={{0,7},{1,6},{2,5},{3,4},{4,3},{5,2},{6,1},{7,0},{8,15},{9,14},{10,... | collective-permute-start | bytes 786440 | tf_op jit(solution)/shard_map/ppermute | solution.py:111
  133.9 39.3 %collective-permute-start.7 = (bf16[512,256]{1,0:T(8,128)(2,1)}, bf16[512,256]{1,0:T(8,128)(2,1)}, u32[]{:S(2)}, u32[]{:S(2)}) collective-permute-start(bf16[512,256]{1,0:T(8,128)(2,1)} %copy-done.14), channel_id=1, source_target_pairs={{0,1},{1,0},{2,3},{3,2},{4,5},{5,4},{6,7},{7,6},{8,9},{9,8},{10,11... | collective-permute-start | bytes 786440 | tf_op jit(solution)/shard_map/ppermute | solution.py:111
  134.9 39.1 %collective-permute-start.8 = (bf16[512,256]{1,0:T(8,128)(2,1)}, bf16[512,256]{1,0:T(8,128)(2,1)}, u32[]{:S(2)}, u32[]{:S(2)}) collective-permute-start(bf16[512,256]{1,0:T(8,128)(2,1)} %copy-done.13), channel_id=1, source_target_pairs={{0,4},{1,5},{2,6},{3,7},{4,0},{5,1},{6,2},{7,3},{8,12},{9,13},{10,... | collective-permute-start | bytes 786440 | tf_op jit(solution)/shard_map/ppermute | solution.py:111
  140.1 33.9 %collective-permute-start.9 = (bf16[512,256]{1,0:T(8,128)(2,1)}, bf16[512,256]{1,0:T(8,128)(2,1)}, u32[]{:S(2)}, u32[]{:S(2)}) collective-permute-start(bf16[512,256]{1,0:T(8,128)(2,1)} %copy-done.12), channel_id=1, source_target_pairs={{0,5},{1,4},{2,7},{3,6},{4,1},{5,0},{6,3},{7,2},{8,13},{9,12},{10,... | collective-permute-start | bytes 786440 | tf_op jit(solution)/shard_map/ppermute | solution.py:111
  140.5 35.1 %copy-start.7 = (bf16[512,256]{1,0:T(8,128)(2,1)S(1)}, bf16[512,256]{1,0:T(8,128)(2,1)}, u32[]{:S(2)}) copy-start(bf16[512,256]{1,0:T(8,128)(2,1)} %copy-done.6) | copy-start | bytes 786436
  170.1 7.6 %collective-permute-start.14 = (bf16[512,256]{1,0:T(8,128)(2,1)S(1)}, bf16[512,256]{1,0:T(8,128)(2,1)S(1)}, u32[]{:S(2)}, u32[]{:S(2)}) collective-permute-start(bf16[512,256]{1,0:T(8,128)(2,1)S(1)} %get-tuple-element.51), channel_id=1, source_target_pairs={{0,1},{1,0},{2,3},{3,2},{4,5},{5,4},{6,7},{7,6},{8,9},{9,8},{10,11... | collective-permute-start | bytes 786440 | tf_op jit(solution)/shard_map/ppermute | solution.py:111
  170.9 8.6 %collective-permute-start.15 = (bf16[512,256]{1,0:T(8,128)(2,1)S(1)}, bf16[512,256]{1,0:T(8,128)(2,1)S(1)}, u32[]{:S(2)}, u32[]{:S(2)}) collective-permute-start(bf16[512,256]{1,0:T(8,128)(2,1)S(1)} %get-tuple-element.52), channel_id=1, source_target_pairs={{0,4},{1,5},{2,6},{3,7},{4,0},{5,1},{6,2},{7,3},{8,12},{9,13},{10,... | collective-permute-start | bytes 786440 | tf_op jit(solution)/shard_map/ppermute | solution.py:111
  173.2 40.2 %collective-permute-start.16 = (bf16[512,256]{1,0:T(8,128)(2,1)}, bf16[512,256]{1,0:T(8,128)(2,1)}, u32[]{:S(2)}, u32[]{:S(2)}) collective-permute-start(bf16[512,256]{1,0:T(8,128)(2,1)} %get-tuple-element.53), channel_id=1, source_target_pairs={{0,5},{1,4},{2,7},{3,6},{4,1},{5,0},{6,3},{7,2},{8,13},{9,12},{10,... | collective-permute-start | bytes 786440 | tf_op jit(solution)/shard_map/ppermute | solution.py:111
  174.0 40.6 %collective-permute-start.17 = (bf16[512,256]{1,0:T(8,128)(2,1)}, bf16[512,256]{1,0:T(8,128)(2,1)}, u32[]{:S(2)}, u32[]{:S(2)}) collective-permute-start(bf16[512,256]{1,0:T(8,128)(2,1)} %get-tuple-element.54), channel_id=1, source_target_pairs={{0,2},{1,3},{2,0},{3,1},{4,6},{5,7},{6,4},{7,5},{8,10},{9,11},{10,... | collective-permute-start | bytes 786440 | tf_op jit(solution)/shard_map/ppermute | solution.py:111
  174.0 43.1 %collective-permute-start.18 = (bf16[512,256]{1,0:T(8,128)(2,1)}, bf16[512,256]{1,0:T(8,128)(2,1)}, u32[]{:S(2)}, u32[]{:S(2)}) collective-permute-start(bf16[512,256]{1,0:T(8,128)(2,1)} %get-tuple-element.55), channel_id=1, source_target_pairs={{0,3},{1,2},{2,1},{3,0},{4,7},{5,6},{6,5},{7,4},{8,11},{9,10},{10,... | collective-permute-start | bytes 786440 | tf_op jit(solution)/shard_map/ppermute | solution.py:111
  177.7 39.4 %collective-permute-start.19 = (bf16[512,256]{1,0:T(8,128)(2,1)}, bf16[512,256]{1,0:T(8,128)(2,1)}, u32[]{:S(2)}, u32[]{:S(2)}) collective-permute-start(bf16[512,256]{1,0:T(8,128)(2,1)} %get-tuple-element.56), channel_id=1, source_target_pairs={{0,6},{1,7},{2,4},{3,5},{4,2},{5,3},{6,0},{7,1},{8,14},{9,15},{10,... | collective-permute-start | bytes 786440 | tf_op jit(solution)/shard_map/ppermute | solution.py:111
  180.1 38.2 %collective-permute-start.20 = (bf16[512,256]{1,0:T(8,128)(2,1)}, bf16[512,256]{1,0:T(8,128)(2,1)}, u32[]{:S(2)}, u32[]{:S(2)}) collective-permute-start(bf16[512,256]{1,0:T(8,128)(2,1)} %get-tuple-element.57), channel_id=1, source_target_pairs={{0,7},{1,6},{2,5},{3,4},{4,3},{5,2},{6,1},{7,0},{8,15},{9,14},{10,... | collective-permute-start | bytes 786440 | tf_op jit(solution)/shard_map/ppermute | solution.py:111
  182.7 36.4 %copy-start.5 = (bf16[512,256]{1,0:T(8,128)(2,1)S(1)}, bf16[512,256]{1,0:T(8,128)(2,1)}, u32[]{:S(2)}) copy-start(bf16[512,256]{1,0:T(8,128)(2,1)} %copy-done.4) | copy-start | bytes 786436
  182.7 36.4 %copy-start.27 = (bf16[512,256]{1,0:T(8,128)(2,1)S(1)}, bf16[512,256]{1,0:T(8,128)(2,1)}, u32[]{:S(2)}) copy-start(bf16[512,256]{1,0:T(8,128)(2,1)} %copy-done.26) | copy-start | bytes 786436
  182.7 36.4 %copy-start.29 = (bf16[512,256]{1,0:T(8,128)(2,1)S(1)}, bf16[512,256]{1,0:T(8,128)(2,1)}, u32[]{:S(2)}) copy-start(bf16[512,256]{1,0:T(8,128)(2,1)} %copy-done.28) | copy-start | bytes 786436
  213.4 40.7 %collective-permute-start.31 = (bf16[512,256]{1,0:T(8,128)(2,1)}, bf16[512,256]{1,0:T(8,128)(2,1)}, u32[]{:S(2)}, u32[]{:S(2)}) collective-permute-start(bf16[512,256]{1,0:T(8,128)(2,1)} %get-tuple-element.68), channel_id=1, source_target_pairs={{0,1},{1,0},{2,3},{3,2},{4,5},{5,4},{6,7},{7,6},{8,9},{9,8},{10,11... | collective-permute-start | bytes 786440 | tf_op jit(solution)/shard_map/ppermute | solution.py:111
  214.6 41.4 %collective-permute-start.32 = (bf16[512,256]{1,0:T(8,128)(2,1)}, bf16[512,256]{1,0:T(8,128)(2,1)}, u32[]{:S(2)}, u32[]{:S(2)}) collective-permute-start(bf16[512,256]{1,0:T(8,128)(2,1)} %get-tuple-element.69), channel_id=1, source_target_pairs={{0,4},{1,5},{2,6},{3,7},{4,0},{5,1},{6,2},{7,3},{8,12},{9,13},{10,... | collective-permute-start | bytes 786440 | tf_op jit(solution)/shard_map/ppermute | solution.py:111
  217.1 39.2 %collective-permute-start.33 = (bf16[512,256]{1,0:T(8,128)(2,1)}, bf16[512,256]{1,0:T(8,128)(2,1)}, u32[]{:S(2)}, u32[]{:S(2)}) collective-permute-start(bf16[512,256]{1,0:T(8,128)(2,1)} %get-tuple-element.70), channel_id=1, source_target_pairs={{0,5},{1,4},{2,7},{3,6},{4,1},{5,0},{6,3},{7,2},{8,13},{9,12},{10,... | collective-permute-start | bytes 786440 | tf_op jit(solution)/shard_map/ppermute | solution.py:111
  217.1 40.1 %collective-permute-start.34 = (bf16[512,256]{1,0:T(8,128)(2,1)}, bf16[512,256]{1,0:T(8,128)(2,1)}, u32[]{:S(2)}, u32[]{:S(2)}) collective-permute-start(bf16[512,256]{1,0:T(8,128)(2,1)} %get-tuple-element.71), channel_id=1, source_target_pairs={{0,2},{1,3},{2,0},{3,1},{4,6},{5,7},{6,4},{7,5},{8,10},{9,11},{10,... | collective-permute-start | bytes 786440 | tf_op jit(solution)/shard_map/ppermute | solution.py:111
  218.4 39.5 %collective-permute-start.35 = (bf16[512,256]{1,0:T(8,128)(2,1)}, bf16[512,256]{1,0:T(8,128)(2,1)}, u32[]{:S(2)}, u32[]{:S(2)}) collective-permute-start(bf16[512,256]{1,0:T(8,128)(2,1)} %get-tuple-element.72), channel_id=1, source_target_pairs={{0,3},{1,2},{2,1},{3,0},{4,7},{5,6},{6,5},{7,4},{8,11},{9,10},{10,... | collective-permute-start | bytes 786440 | tf_op jit(solution)/shard_map/ppermute | solution.py:111
  254.1 7.7 %collective-permute-start.36 = (bf16[512,256]{1,0:T(8,128)(2,1)S(1)}, bf16[512,256]{1,0:T(8,128)(2,1)S(1)}, u32[]{:S(2)}, u32[]{:S(2)}) collective-permute-start(bf16[512,256]{1,0:T(8,128)(2,1)S(1)} %copy-done.11), channel_id=1, source_target_pairs={{0,6},{1,7},{2,4},{3,5},{4,2},{5,3},{6,0},{7,1},{8,14},{9,15},{10,... | collective-permute-start | bytes 786440 | tf_op jit(solution)/shard_map/ppermute | solution.py:111
  255.9 11.8 %collective-permute-start.37 = (bf16[512,256]{1,0:T(8,128)(2,1)S(1)}, bf16[512,256]{1,0:T(8,128)(2,1)S(1)}, u32[]{:S(2)}, u32[]{:S(2)}) collective-permute-start(bf16[512,256]{1,0:T(8,128)(2,1)S(1)} %copy-done.9), channel_id=1, source_target_pairs={{0,7},{1,6},{2,5},{3,4},{4,3},{5,2},{6,1},{7,0},{8,15},{9,14},{10,... | collective-permute-start | bytes 786440 | tf_op jit(solution)/shard_map/ppermute | solution.py:111
  256.3 14.5 %collective-permute-start.22 = (bf16[512,256]{1,0:T(8,128)(2,1)S(1)}, bf16[512,256]{1,0:T(8,128)(2,1)S(1)}, u32[]{:S(2)}, u32[]{:S(2)}) collective-permute-start(bf16[512,256]{1,0:T(8,128)(2,1)S(1)} %get-tuple-element.60), channel_id=1, source_target_pairs={{0,1},{1,0},{2,3},{3,2},{4,5},{5,4},{6,7},{7,6},{8,9},{9,8},{10,11... | collective-permute-start | bytes 786440 | tf_op jit(solution)/shard_map/ppermute | solution.py:111
  257.3 38.6 %collective-permute-start.21 = (bf16[512,512]{0,1:T(8,128)(2,1)S(1)}, bf16[512,512]{0,1:T(8,128)(2,1)S(1)}, u32[]{:S(2)}, u32[]{:S(2)}) collective-permute-start(bf16[512,512]{0,1:T(8,128)(2,1)S(1)} %slice_bitcast_fusion), channel_id=1, source_target_pairs={{0,1},{1,0},{2,3},{3,2},{4,5},{5,4},{6,7},{7,6},{8,9},{9,8},{10,11... | collective-permute-start | bytes 1572872 | tf_op jit(solution)/shard_map/ppermute | solution.py:111
  257.9 18.3 %collective-permute-start.23 = (bf16[512,256]{1,0:T(8,128)(2,1)S(1)}, bf16[512,256]{1,0:T(8,128)(2,1)S(1)}, u32[]{:S(2)}, u32[]{:S(2)}) collective-permute-start(bf16[512,256]{1,0:T(8,128)(2,1)S(1)} %get-tuple-element.61), channel_id=1, source_target_pairs={{0,4},{1,5},{2,6},{3,7},{4,0},{5,1},{6,2},{7,3},{8,12},{9,13},{10,... | collective-permute-start | bytes 786440 | tf_op jit(solution)/shard_map/ppermute | solution.py:111
  261.7 18.7 %collective-permute-start.24 = (bf16[512,256]{1,0:T(8,128)(2,1)S(1)}, bf16[512,256]{1,0:T(8,128)(2,1)S(1)}, u32[]{:S(2)}, u32[]{:S(2)}) collective-permute-start(bf16[512,256]{1,0:T(8,128)(2,1)S(1)} %get-tuple-element.62), channel_id=1, source_target_pairs={{0,5},{1,4},{2,7},{3,6},{4,1},{5,0},{6,3},{7,2},{8,13},{9,12},{10,... | collective-permute-start | bytes 786440 | tf_op jit(solution)/shard_map/ppermute | solution.py:111
  267.8 12.7 %collective-permute-start.25 = (bf16[512,256]{1,0:T(8,128)(2,1)S(1)}, bf16[512,256]{1,0:T(8,128)(2,1)S(1)}, u32[]{:S(2)}, u32[]{:S(2)}) collective-permute-start(bf16[512,256]{1,0:T(8,128)(2,1)S(1)} %get-tuple-element.63), channel_id=1, source_target_pairs={{0,2},{1,3},{2,0},{3,1},{4,6},{5,7},{6,4},{7,5},{8,10},{9,11},{10,... | collective-permute-start | bytes 786440 | tf_op jit(solution)/shard_map/ppermute | solution.py:111
  270.8 21.6 %collective-permute-start.26 = (bf16[512,256]{1,0:T(8,128)(2,1)S(1)}, bf16[512,256]{1,0:T(8,128)(2,1)S(1)}, u32[]{:S(2)}, u32[]{:S(2)}) collective-permute-start(bf16[512,256]{1,0:T(8,128)(2,1)S(1)} %get-tuple-element.64), channel_id=1, source_target_pairs={{0,3},{1,2},{2,1},{3,0},{4,7},{5,6},{6,5},{7,4},{8,11},{9,10},{10,... | collective-permute-start | bytes 786440 | tf_op jit(solution)/shard_map/ppermute | solution.py:111
  276.2 25.4 %collective-permute-start.30 = (bf16[512,256]{1,0:T(8,128)(2,1)}, bf16[512,256]{1,0:T(8,128)(2,1)}, u32[]{:S(2)}, u32[]{:S(2)}) collective-permute-start(bf16[512,256]{1,0:T(8,128)(2,1)} %add_convert_fusion.2.refs_0_), channel_id=1, source_target_pairs={{0,16},{1,17},{2,18},{3,19},{4,20},{5,21},{6,22},{7,23},{8,24},{9,... | collective-permute-start | bytes 786440 | tf_op jit(solution)/shard_map/ppermute | solution.py:111
  280.5 21.1 %collective-permute-start.29 = (bf16[512,256]{1,0:T(8,128)(2,1)S(1)}, bf16[512,256]{1,0:T(8,128)(2,1)}, u32[]{:S(2)}, u32[]{:S(2)}) collective-permute-start(bf16[512,256]{1,0:T(8,128)(2,1)S(1)} %add_convert_fusion.3.refs_0_), channel_id=1, source_target_pairs={{0,8},{1,9},{2,10},{3,11},{4,12},{5,13},{6,14},{7,15},{8,0},{9,1},... | collective-permute-start | bytes 786440 | tf_op jit(solution)/shard_map/ppermute | solution.py:111
  280.5 16.9 %collective-permute-start.27 = (bf16[512,256]{1,0:T(8,128)(2,1)}, bf16[512,256]{1,0:T(8,128)(2,1)}, u32[]{:S(2)}, u32[]{:S(2)}) collective-permute-start(bf16[512,256]{1,0:T(8,128)(2,1)} %get-tuple-element.65), channel_id=1, source_target_pairs={{0,6},{1,7},{2,4},{3,5},{4,2},{5,3},{6,0},{7,1},{8,14},{9,15},{10,... | collective-permute-start | bytes 786440 | tf_op jit(solution)/shard_map/ppermute | solution.py:111
  292.4 9.2 %collective-permute-start.28 = (bf16[512,256]{1,0:T(8,128)(2,1)}, bf16[512,256]{1,0:T(8,128)(2,1)}, u32[]{:S(2)}, u32[]{:S(2)}) collective-permute-start(bf16[512,256]{1,0:T(8,128)(2,1)} %get-tuple-element.66), channel_id=1, source_target_pairs={{0,7},{1,6},{2,5},{3,4},{4,3},{5,2},{6,1},{7,0},{8,15},{9,14},{10,... | collective-permute-start | bytes 786440 | tf_op jit(solution)/shard_map/ppermute | solution.py:111
  295.9 7.9 %collective-permute-start.38 = (bf16[512,256]{1,0:T(8,128)(2,1)}, bf16[512,256]{1,0:T(8,128)(2,1)}, u32[]{:S(2)}, u32[]{:S(2)}) collective-permute-start(bf16[512,256]{1,0:T(8,128)(2,1)} %add_convert_fusion.1), channel_id=1, source_target_pairs={{0,24},{1,25},{2,26},{3,27},{4,28},{5,29},{6,30},{7,31},{8,16},{9,... | collective-permute-start | bytes 786440 | tf_op jit(solution)/shard_map/ppermute | solution.py:111
  (34 other events, 204.0 us)
Sparse Core Ops, SparseCore 0:
  29.4 24.9 all-gather.10
  56.0 23.2 all-gather.8
  89.1 21.2 all-gather.6
  132.0 31.5 all-gather.4
